TPU v7x, 32 devices: a whole 2x2x4 slice. The times are simulated.
32 devices in a mesh: section: 4 (over y, core), fsdp: 2 (over x), seq: 4 (over z).
Axes of the slice: x: 2, y: 2, z: 4, core: 2. Of those that a mesh axis runs over, the one named last changes fastest.
Arguments:
- hidden: bfloat16 [4, 2048, 8192], P('section', ('fsdp', 'seq')), may hold values from -6 to 6
- queries: bfloat16 [4, 2048, 4096], P('section', ('fsdp', 'seq')), may hold values from -6 to 6
- kv_weight: bfloat16 [4, 8192, 1024], P('section', ('fsdp', 'seq')), may hold values from -0.0625 to 0.0625
- readout: float32 [4, 4096], P('section'), may hold values from -6 to 6
- segments: int32 [2, 1024], P('fsdp'), may hold values from 0 to 3, never falling along the last dimension, each value on 1 to 512 neighbouring positions
- block_mask: int32 [2, 8, 8], P('fsdp', 'seq'), may hold values 0 or 1
- response: int32 [2048], P(('fsdp', 'seq')), may hold values 0 or 1
Outputs:
- scores: float32 [4, 2048], P('section', ('fsdp', 'seq'))
- query_grad: bfloat16 [4, 2048, 4096], P('section', ('fsdp', 'seq'))
All inputs are finite; a program needn't handle non-finite values. No bound on the sum of `block_mask` or of `response` on one device may be relied on, other than what follows from the above.
Results may differ from a plain program's by a relative error of at most 0.02.
Values may be sent and summed in bfloat16 or wider, within the bound.
A program may use at most 128 MiB of HBM per device.

v0:
```python
import math

import jax
import jax.numpy as jnp
from jax import lax
from jax.sharding import PartitionSpec as P

QH = 32
KVH = 4
HD = 128
BLK = 128


penalty_weight = 0.5


def on_device(hidden, queries, kv_weight, readout, segments, block_mask, response):
    local_rows = hidden[0]
    row_count = local_rows.shape[0]
    kv_width = KVH * HD
    group_size = QH // KVH
    score_scale = 1.0 / math.sqrt(HD)
    fsdp_count = lax.axis_size("fsdp")
    seq_count = lax.axis_size("seq")
    slab_rows = kv_weight.shape[1]
    split_rows = local_rows.reshape(row_count, fsdp_count, seq_count, slab_rows)
    traded = lax.all_to_all(split_rows, "seq", split_axis=2, concat_axis=0, tiled=True)
    sequence_rows = traded.reshape(traded.shape[0], fsdp_count * slab_rows)
    weight_part = lax.all_gather(kv_weight[0], "fsdp", axis=0, tiled=True)
    partial_kv = jnp.dot(sequence_rows, weight_part, preferred_element_type=jnp.float32)
    whole_kv = lax.psum(partial_kv, "seq").astype(jnp.bfloat16)
    query_rows = queries[0].reshape(row_count, KVH, group_size, HD)
    read_gains = readout[0].reshape(KVH, group_size, HD)
    seq_index = lax.axis_index("seq")
    query_pos = seq_index * row_count + jnp.arange(row_count, dtype=jnp.int32)
    doc_ids = segments[0]
    query_docs = lax.dynamic_slice_in_dim(doc_ids, seq_index * row_count, row_count)
    mask_rows = block_mask[0]
    mask_width = row_count // BLK

    def key_block(block_number, carry):
        den_sum, value_sum, first_sum, second_sum = carry
        start = (block_number * row_count).astype(jnp.int32)
        block_kv = lax.dynamic_slice_in_dim(whole_kv, start, row_count, 0)
        block_keys = block_kv[:, :kv_width].reshape(row_count, KVH, HD)
        block_values = block_kv[:, kv_width:].reshape(row_count, KVH, HD)
        key_pos = start + jnp.arange(row_count, dtype=jnp.int32)
        key_docs = lax.dynamic_slice_in_dim(doc_ids, start, row_count)
        mask_cols = lax.dynamic_slice_in_dim(mask_rows, start // BLK, mask_width, 1)
        block_table = jnp.repeat(jnp.repeat(mask_cols, BLK, axis=0), BLK, axis=1)
        allowed = (
            (query_docs[:, None] == key_docs[None, :])
            & (key_pos[None, :] <= query_pos[:, None])
            & ((block_table == 1) | (query_pos[:, None] // BLK == key_pos[None, :] // BLK))
        )
        logits = (
            jnp.einsum("ikgd,jkd->kgij", query_rows, block_keys, preferred_element_type=jnp.float32)
            * score_scale
        )
        weights = jnp.where(allowed[None, None], jnp.exp(logits), 0.0)
        den_sum = den_sum + jnp.transpose(jnp.sum(weights, axis=-1), (2, 0, 1))
        rounded = weights.astype(jnp.bfloat16)
        value_sum = value_sum + jnp.einsum(
            "kgij,jkd->ikgd", rounded, block_values, preferred_element_type=jnp.float32
        )
        value_gain = jnp.einsum("jkd,kgd->jkg", block_values.astype(jnp.float32), read_gains)
        scaled = (weights * jnp.transpose(value_gain, (1, 2, 0))[:, :, None, :]).astype(
            jnp.bfloat16
        )
        first_sum = first_sum + jnp.einsum(
            "kgij,jkd->ikgd", scaled, block_keys, preferred_element_type=jnp.float32
        )
        second_sum = second_sum + jnp.einsum(
            "kgij,jkd->ikgd", rounded, block_keys, preferred_element_type=jnp.float32
        )
        return (den_sum, value_sum, first_sum, second_sum)

    empty_den = jnp.zeros((row_count, KVH, group_size), jnp.float32)
    empty_acc = jnp.zeros((row_count, KVH, group_size, HD), jnp.float32)
    denominator, value_sum, first_sum, second_sum = lax.fori_loop(
        0, seq_index + 1, key_block, (empty_den, empty_acc, empty_acc, empty_acc)
    )
    attended = value_sum / denominator[..., None]
    head_scores = jnp.sum(attended * read_gains, axis=-1)
    token_scores = jnp.sum(head_scores, axis=(1, 2))
    joined = lax.all_gather(token_scores[None, :], "section", axis=0, tiled=True)
    section_index = lax.axis_index("section")
    actor_part = (section_index == 0).astype(jnp.float32)
    critic_part = (section_index == 3).astype(jnp.float32)
    live_rows = response.astype(jnp.float32)
    actor_term = penalty_weight * (joined[0] - joined[1]) - (joined[2] - joined[3])
    critic_term = joined[3] - joined[2]
    loss_grad = live_rows * (actor_part * actor_term + critic_part * critic_term)
    factor = score_scale * loss_grad[:, None, None] / denominator
    result = factor[..., None] * (first_sum - head_scores[..., None] * second_sum)
    query_grad = result.reshape(row_count, QH * HD).astype(jnp.bfloat16)
    return (token_scores[None, :], query_grad[None])


def solution(mesh):
    placed = (
        P("section", ("fsdp", "seq"), None),
        P("section", ("fsdp", "seq"), None),
        P("section", ("fsdp", "seq"), None),
        P("section", None),
        P("fsdp", None),
        P("fsdp", "seq", None),
        P(("fsdp", "seq")),
    )
    return jax.shard_map(
        on_device,
        mesh=mesh,
        in_specs=placed,
        out_specs=(P("section", ("fsdp", "seq")), P("section", ("fsdp", "seq"), None)),
        check_vma=False,
    )
```

profile of v0, /device:TPU:25, one launch (start us, length us, event | category | flops | bytes accessed | tf_op | source)
XLA Modules:
  0.0 403.9 jit_solution(7328042318394625601)
XLA Ops:
  7.2 7.8 %reshape_squeeze.9 = bf16[256,2,4,1024]{3,2,1,0:T(4,128)(2,1)} reshape(bf16[1,256,8192]{2,1,0:T(8,128)(2,1)} %param.9) | data formatting | bytes 8388608 | tf_op jit(solution)/shard_map/reshape;squeeze | solution.py:26
  15.0 7.4 %copy.32 = bf16[256,2,4,1024]{3,1,0,2:T(2,128)(2,1)} copy(bf16[256,2,4,1024]{3,2,1,0:T(4,128)(2,1)} %reshape_squeeze.9) | data formatting | bytes 8388608 | tf_op jit(solution)/shard_map/reshape;squeeze | solution.py:26
  22.4 4.9 %all-to-all-start = ((bf16[256,2,4,1024]{3,1,0,2:T(2,128)(2,1)}), bf16[256,2,4,1024]{3,1,0,2:T(2,128)(2,1)}, u32[]{:S(2)}, u32[]{:S(2)}) async-start(bf16[256,2,4,1024]{3,1,0,2:T(2,128)(2,1)} %copy.32), calls=%async_computation | async-start | bytes 8388608 | tf_op jit(solution)/shard_map/all_to_all | solution.py:27
  27.3 0.7 all-gather.5.cloned.1.call-update
  28.0 3.3 copy.33
  31.3 2.4 copy.36
  33.7 83.6 %all-to-all-done = bf16[256,2,4,1024]{3,1,0,2:T(2,128)(2,1)} async-done(((bf16[256,2,4,1024]{3,1,0,2:T(2,128)(2,1)}), bf16[256,2,4,1024]{3,1,0,2:T(2,128)(2,1)}, u32[]{:S(2)}, u32[]{:S(2)}) %all-to-all-start) | async-done | bytes 4194336 | tf_op jit(solution)/shard_map/all_to_all | solution.py:27
  117.3 5.6 %copy.53 = bf16[128,8,2,1024]{3,1,2,0:T(8,128)(2,1)} copy(bf16[128,8,2,1024]{3,2,1,0:T(2,128)(2,1)} %bitcast.42) | data formatting | bytes 8388608
  122.9 9.9 %fusion.24 = f32[1024,1024]{1,0:T(8,128)} fusion(bf16[1024,2048]{1,0:T(8,128)(2,1)} %bitcast.131, bf16[1,2048,1024]{2,1,0:T(8,128)(2,1)} %all-gather.5.cloned.1.call-done), kind=kOutput, calls=%fused_computation.44 | convolution fusion | flops 4294967296 | bytes 12582912 | tf_op jit(solution)/shard_map/dot_general | solution.py:30
  132.8 141.0 %all-reduce.1 = bf16[1024,1024]{1,0:T(8,128)(2,1)S(1)} all-reduce(f32[1024,1024]{1,0:T(8,128)} %fusion.24), channel_id=1, replica_groups=mesh['section'=4,'fsdp'=2,'seq'=4] {'seq'}, use_global_device_ids=true, to_apply=%region_0.0 | all-reduce | flops 1048576 | bytes 6291456 | tf_op jit(solution)/shard_map/psum | solution.py:31
  273.8 2.5 broadcast_in_dim.59
  276.3 2.4 broadcast_in_dim.59.clone
  278.7 2.4 broadcast_in_dim.59.clone.1
  281.2 97.1 %while.21 = (s32[]{:T(128)}, f32[256,4,8]{0,2,1:T(8,128)S(1)}, f32[256,4,8,128]{0,3,2,1:T(8,128)}, f32[256,4,8,128]{0,3,2,1:T(8,128)}, f32[256,4,8,128]{0,3,2,1:...) while((s32[]{:T(128)}, f32[256,4,8]{0,2,1:T(8,128)S(1)}, ...), condition=%wide.region_3.4_spmd.clone.clone, body=%wide.region_1.3_spmd.clone.clone.sunk | while | flops 2180391424 | bytes 157050080 | solution.py:80
  281.6 0.2 fusion.63
  281.9 6.7 %fusion.65 = (f32[4,8,256]{2,1,0:T(8,128)S(1)}, f32[4,256,256,8]{2,1,3,0:T(8,128)}) fusion(pred[256,256]{0,1:T(8,128)(4,1)S(1)} %fusion.63, bf16[256,4,128,1]{0,2,3,1:T(8,128)(2,1)S(1)} %bitcast.125, bf16[256,4,8,128]{3,0,2,1:T(8,128)(2,1)} %get-tuple-element.523), kind=kOutput, calls=%fused_computation.6.clone.1 | convolution fusion | flops 543154176 | bytes 10846208 | tf_op jit(solution)/shard_map/while/body/ikgd,jkd->kgij/dot_general | solution.py:57
  288.9 8.7 %bitcast_add_fusion.9 = f32[256,4,8,128]{0,3,2,1:T(8,128)} fusion(f32[256,4,8,128]{0,3,2,1:T(8,128)} %get-tuple-element.493, bf16[256,4,128,1]{0,2,3,1:T(8,128)(2,1)S(1)} %bitcast.128, f32[4,256,256,8]{2,1,3,0:T(8,128)} %get-tuple-element.468, pred[256,256]{0,1:T(8,128)(4,1)S(1)} %fusion.63), kind=kOutput, calls=%fused_computation.10.clone.1 | convolution fusion | flops 544210944 | bytes 17104896 | tf_op jit(solution)/shard_map/while/body/kgij,jkd->ikgd/dot_general | solution.py:63
  297.6 0.1 convolution_bitcast_fusion.2
  297.7 0.9 copy-done.1
  298.6 2.7 bitcast_add_fusion.10
  301.3 2.1 bitcast_add_fusion.11
  303.5 2.0 copy-done.4
  305.9 0.2 fusion.63
  306.2 6.7 %fusion.65 = (f32[4,8,256]{2,1,0:T(8,128)S(1)}, f32[4,256,256,8]{2,1,3,0:T(8,128)}) fusion(pred[256,256]{0,1:T(8,128)(4,1)S(1)} %fusion.63, bf16[256,4,128,1]{0,2,3,1:T(8,128)(2,1)S(1)} %bitcast.125, bf16[256,4,8,128]{3,0,2,1:T(8,128)(2,1)} %get-tuple-element.523), kind=kOutput, calls=%fused_computation.6.clone.1 | convolution fusion | flops 543154176 | bytes 10846208 | tf_op jit(solution)/shard_map/while/body/ikgd,jkd->kgij/dot_general | solution.py:57
  313.2 8.7 %bitcast_add_fusion.9 = f32[256,4,8,128]{0,3,2,1:T(8,128)} fusion(f32[256,4,8,128]{0,3,2,1:T(8,128)} %get-tuple-element.493, bf16[256,4,128,1]{0,2,3,1:T(8,128)(2,1)S(1)} %bitcast.128, f32[4,256,256,8]{2,1,3,0:T(8,128)} %get-tuple-element.468, pred[256,256]{0,1:T(8,128)(4,1)S(1)} %fusion.63), kind=kOutput, calls=%fused_computation.10.clone.1 | convolution fusion | flops 544210944 | bytes 17104896 | tf_op jit(solution)/shard_map/while/body/kgij,jkd->ikgd/dot_general | solution.py:63
  322.0 0.9 copy-done.1
  322.9 2.7 bitcast_add_fusion.10
  325.6 2.1 bitcast_add_fusion.11
  327.8 2.0 copy-done.4
  330.1 0.2 fusion.63
  330.5 6.7 %fusion.65 = (f32[4,8,256]{2,1,0:T(8,128)S(1)}, f32[4,256,256,8]{2,1,3,0:T(8,128)}) fusion(pred[256,256]{0,1:T(8,128)(4,1)S(1)} %fusion.63, bf16[256,4,128,1]{0,2,3,1:T(8,128)(2,1)S(1)} %bitcast.125, bf16[256,4,8,128]{3,0,2,1:T(8,128)(2,1)} %get-tuple-element.523), kind=kOutput, calls=%fused_computation.6.clone.1 | convolution fusion | flops 543154176 | bytes 10846208 | tf_op jit(solution)/shard_map/while/body/ikgd,jkd->kgij/dot_general | solution.py:57
  337.4 8.7 %bitcast_add_fusion.9 = f32[256,4,8,128]{0,3,2,1:T(8,128)} fusion(f32[256,4,8,128]{0,3,2,1:T(8,128)} %get-tuple-element.493, bf16[256,4,128,1]{0,2,3,1:T(8,128)(2,1)S(1)} %bitcast.128, f32[4,256,256,8]{2,1,3,0:T(8,128)} %get-tuple-element.468, pred[256,256]{0,1:T(8,128)(4,1)S(1)} %fusion.63), kind=kOutput, calls=%fused_computation.10.clone.1 | convolution fusion | flops 544210944 | bytes 17104896 | tf_op jit(solution)/shard_map/while/body/kgij,jkd->ikgd/dot_general | solution.py:63
  346.3 0.9 copy-done.1
  347.2 2.7 bitcast_add_fusion.10
  349.9 2.1 bitcast_add_fusion.11
  352.0 2.0 copy-done.4
  354.4 0.2 fusion.63
  354.8 6.7 %fusion.65 = (f32[4,8,256]{2,1,0:T(8,128)S(1)}, f32[4,256,256,8]{2,1,3,0:T(8,128)}) fusion(pred[256,256]{0,1:T(8,128)(4,1)S(1)} %fusion.63, bf16[256,4,128,1]{0,2,3,1:T(8,128)(2,1)S(1)} %bitcast.125, bf16[256,4,8,128]{3,0,2,1:T(8,128)(2,1)} %get-tuple-element.523), kind=kOutput, calls=%fused_computation.6.clone.1 | convolution fusion | flops 543154176 | bytes 10846208 | tf_op jit(solution)/shard_map/while/body/ikgd,jkd->kgij/dot_general | solution.py:57
  361.7 8.7 %bitcast_add_fusion.9 = f32[256,4,8,128]{0,3,2,1:T(8,128)} fusion(f32[256,4,8,128]{0,3,2,1:T(8,128)} %get-tuple-element.493, bf16[256,4,128,1]{0,2,3,1:T(8,128)(2,1)S(1)} %bitcast.128, f32[4,256,256,8]{2,1,3,0:T(8,128)} %get-tuple-element.468, pred[256,256]{0,1:T(8,128)(4,1)S(1)} %fusion.63), kind=kOutput, calls=%fused_computation.10.clone.1 | convolution fusion | flops 544210944 | bytes 17104896 | tf_op jit(solution)/shard_map/while/body/kgij,jkd->ikgd/dot_general | solution.py:63
  370.4 0.1 convolution_bitcast_fusion.2
  370.5 0.9 copy-done.1
  371.4 2.7 bitcast_add_fusion.10
  374.2 2.1 bitcast_add_fusion.11
  376.3 2.0 copy-done.4
  378.3 2.7 fusion.30
  381.0 9.0 %all-gather.2 = f32[4,1,256]{2,1,0:T(1,128)S(1)} all-gather(f32[1,1,256]{2,1,0:T(1,128)S(1)} %bitcast.141), channel_id=3, replica_groups=mesh['section'=4,'fsdp'=2,'seq'=4] {'section'}, dimensions={0}, use_global_device_ids=true | all-gather | bytes 5120 | tf_op jit(solution)/shard_map/all_gather | solution.py:86
  390.1 4.1 %multiply_convert_fusion.4 = bf16[256,4,8,128]{0,3,2,1:T(8,128)(2,1)S(1)} fusion(f32[256,4,8,128]{0,3,2,1:T(8,128)} %get-tuple-element.226, f32[256,4,8,128]{0,3,2,1:T(8,128)} %get-tuple-element.227, f32[256,4,8]{0,2,1:T(8,128)S(1)} %broadcast_divide_fusion, f32[256,4,8,128]{0,3,2,1:T(8,128)S(1)} %copy-done, f32[4,8,128]{2,1,0:T(8,128)S(1)} %bitcast.136, ...), kind=kOutput, calls=%fused_computation.46 | output fusion | flops 6299775 | bytes 14761984 | tf_op jit(solution)/shard_map/mul | solution.py:95
  394.2 2.9 copy.45
  (122 shorter events, 3.3 us)
Async XLA Ops:
  22.4 95.0 %all-to-all-start = ((bf16[256,2,4,1024]{3,1,0,2:T(2,128)(2,1)}), bf16[256,2,4,1024]{3,1,0,2:T(2,128)(2,1)}, u32[]{:S(2)}, u32[]{:S(2)}) async-start(bf16[256,2,4,1024]{3,1,0,2:T(2,128)(2,1)} %copy.32), calls=%async_computation | async-start | bytes 8388608 | tf_op jit(solution)/shard_map/all_to_all | solution.py:27
  27.2 95.7 %all-gather.5.cloned.1.call-start = ((), (), s32[]{:S(2)}) async-start(), calls=%async_computation.1 | async-start | bytes 6291456 | tf_op jit(solution)/shard_map/all_gather | solution.py:29
  28.0 5.7 %copy-start.5 = (f32[1,4096]{1,0:T(1,128)S(1)}, f32[1,4096]{1,0:T(1,128)}, u32[]{:S(2)}) copy-start(f32[1,4096]{1,0:T(1,128)} %param.12) | copy-start | bytes 49156
  28.0 5.7 %copy-start.7 = (s32[1,1024]{1,0:T(1,128)S(1)}, s32[1,1024]{1,0:T(1,128)}, u32[]{:S(2)}) copy-start(s32[1,1024]{1,0:T(1,128)} %param.13) | copy-start | bytes 12292
  276.3 4.9 %copy-start.6 = (s32[1,2,8]{2,1,0:T(2,128)S(1)}, s32[1,2,8]{2,1,0:T(2,128)}, u32[]{:S(2)}) copy-start(s32[1,2,8]{2,1,0:T(2,128)} %param.14) | copy-start | bytes 196
  288.8 8.9 %slice-start = ((s8[8388608]{0:T(1024)(128)(4,1)}), s8[4194304]{0:T(1024)(128)(4,1)S(1)}, s32[]{:S(2)}) async-start(s8[8388608]{0:T(1024)(128)(4,1)} %bitcast.123), calls=%async_computation.2 | async-start | bytes 8388608 | tf_op jit(solution)/shard_map/while
  288.9 8.9 %slice-start.1 = ((s8[8388608]{0:T(1024)(128)(4,1)}), s8[4194304]{0:T(1024)(128)(4,1)S(1)}, s32[]{:S(2)}) async-start(s8[8388608]{0:T(1024)(128)(4,1)} %bitcast.123), calls=%async_computation.3 | async-start | bytes 8388608 | tf_op jit(solution)/shard_map/while
  288.9 9.7 %copy-start.1 = (f32[256,4,8,128]{0,3,2,1:T(8,128)S(1)}, f32[256,4,8,128]{0,3,2,1:T(8,128)}, u32[]{:S(2)}) copy-start(f32[256,4,8,128]{0,3,2,1:T(8,128)} %get-tuple-element.494) | copy-start | bytes 12582916 | tf_op jit(solution)/shard_map/while
  298.6 2.7 copy-start.3
  301.3 2.2 copy-start.2
  303.5 2.0 copy-start.4
  313.1 8.9 %slice-start = ((s8[8388608]{0:T(1024)(128)(4,1)}), s8[4194304]{0:T(1024)(128)(4,1)S(1)}, s32[]{:S(2)}) async-start(s8[8388608]{0:T(1024)(128)(4,1)} %bitcast.123), calls=%async_computation.2 | async-start | bytes 8388608 | tf_op jit(solution)/shard_map/while
  313.1 8.9 %slice-start.1 = ((s8[8388608]{0:T(1024)(128)(4,1)}), s8[4194304]{0:T(1024)(128)(4,1)S(1)}, s32[]{:S(2)}) async-start(s8[8388608]{0:T(1024)(128)(4,1)} %bitcast.123), calls=%async_computation.3 | async-start | bytes 8388608 | tf_op jit(solution)/shard_map/while
  313.1 9.7 %copy-start.1 = (f32[256,4,8,128]{0,3,2,1:T(8,128)S(1)}, f32[256,4,8,128]{0,3,2,1:T(8,128)}, u32[]{:S(2)}) copy-start(f32[256,4,8,128]{0,3,2,1:T(8,128)} %get-tuple-element.494) | copy-start | bytes 12582916 | tf_op jit(solution)/shard_map/while
  322.9 2.7 copy-start.3
  325.6 2.2 copy-start.2
  327.8 2.0 copy-start.4
  337.4 8.9 %slice-start = ((s8[8388608]{0:T(1024)(128)(4,1)}), s8[4194304]{0:T(1024)(128)(4,1)S(1)}, s32[]{:S(2)}) async-start(s8[8388608]{0:T(1024)(128)(4,1)} %bitcast.123), calls=%async_computation.2 | async-start | bytes 8388608 | tf_op jit(solution)/shard_map/while
  337.4 8.9 %slice-start.1 = ((s8[8388608]{0:T(1024)(128)(4,1)}), s8[4194304]{0:T(1024)(128)(4,1)S(1)}, s32[]{:S(2)}) async-start(s8[8388608]{0:T(1024)(128)(4,1)} %bitcast.123), calls=%async_computation.3 | async-start | bytes 8388608 | tf_op jit(solution)/shard_map/while
  337.4 9.7 %copy-start.1 = (f32[256,4,8,128]{0,3,2,1:T(8,128)S(1)}, f32[256,4,8,128]{0,3,2,1:T(8,128)}, u32[]{:S(2)}) copy-start(f32[256,4,8,128]{0,3,2,1:T(8,128)} %get-tuple-element.494) | copy-start | bytes 12582916 | tf_op jit(solution)/shard_map/while
  347.2 2.7 copy-start.3
  349.9 2.2 copy-start.2
  352.0 2.0 copy-start.4
  361.7 8.9 %slice-start = ((s8[8388608]{0:T(1024)(128)(4,1)}), s8[4194304]{0:T(1024)(128)(4,1)S(1)}, s32[]{:S(2)}) async-start(s8[8388608]{0:T(1024)(128)(4,1)} %bitcast.123), calls=%async_computation.2 | async-start | bytes 8388608 | tf_op jit(solution)/shard_map/while
  361.7 8.9 %slice-start.1 = ((s8[8388608]{0:T(1024)(128)(4,1)}), s8[4194304]{0:T(1024)(128)(4,1)S(1)}, s32[]{:S(2)}) async-start(s8[8388608]{0:T(1024)(128)(4,1)} %bitcast.123), calls=%async_computation.3 | async-start | bytes 8388608 | tf_op jit(solution)/shard_map/while
  361.7 9.7 %copy-start.1 = (f32[256,4,8,128]{0,3,2,1:T(8,128)S(1)}, f32[256,4,8,128]{0,3,2,1:T(8,128)}, u32[]{:S(2)}) copy-start(f32[256,4,8,128]{0,3,2,1:T(8,128)} %get-tuple-element.494) | copy-start | bytes 12582916 | tf_op jit(solution)/shard_map/while
  371.4 2.7 copy-start.3
  374.1 2.2 copy-start.2
  376.3 2.0 copy-start.4
  378.3 11.8 %copy-start.9 = (s32[256]{0:T(256)S(1)}, s32[256]{0:T(256)}, u32[]{:S(2)}) copy-start(s32[256]{0:T(256)} %param.15) | copy-start | bytes 3076
  378.3 11.8 %copy-start = (f32[256,4,8,128]{0,3,2,1:T(8,128)S(1)}, f32[256,4,8,128]{0,3,2,1:T(8,128)}, u32[]{:S(2)}) copy-start(f32[256,4,8,128]{0,3,2,1:T(8,128)} %get-tuple-element.224) | copy-start | bytes 12582916
  381.0 13.2 %copy-start.8 = (f32[256]{0:T(256)}, f32[256]{0:T(256)S(1)}, u32[]{:S(2)}) copy-start(f32[256]{0:T(256)S(1)} %fusion.30) | copy-start | bytes 3076
Sparse Core Ops, SparseCore 0:
  29.6 57.9 all-gather.4
where the time goes:
time: 405 us; the launch traced here: 404 us
  blocking collectives  150 us (37%)
  matrix products  91.6 us (23%)
  waiting for transfers between devices  84.3 us (21%)
  local copies, waits for them, and re-layouts  50.7 us (13%)
  between operations  14.2 us (4%)
  other arithmetic  7.84 us (2%)
  starting transfers between devices  4.92 us (1%)
    psum x1, blocking collectives, on_device(): whole_kv = lax.psum(partial_kv, 'seq').astype(jnp.bfloat16)  141 us
    all_to_all x1, waiting for transfers between devices, on_device(): lax.all_to_all(split_rows, 'seq', split_axis=2, concat_axis=0, tiled=True)  83.6 us
    dot_general x4, matrix products, key_block(): jnp.einsum('kgij,jkd->ikgd', rounded, block_values, preferred_element_typ...  34.7 us
    dot_general x4, matrix products, key_block(): jnp.einsum('ikgd,jkd->kgij', query_rows, block_keys, preferred_element_ty...  27 us
    another operation x2, local copies, waits for them, and re-layouts, on_device(): split_rows = local_rows.reshape(row_count, fsdp_count, seq_count, slab_rows)  15.2 us
    while x64, local copies, waits for them, and re-layouts  12.9 us
    unnamed x15, local copies, waits for them, and re-layouts  11.3 us
    dot_general x4, matrix products, key_block(): jnp.einsum('kgij,jkd->ikgd', scaled, block_keys, preferred_element_type=j...  10.8 us
  transfers between devices with their start and end apart: 2, of which 1 were waited for; matrix products, arithmetic and copies ran while one was open for 3% of the time, Pallas kernels for 0%

commit v1 on v0

v1 whole, which is shorter than its diff:
```python
import functools
import math

import jax
import jax.numpy as jnp
from jax import lax
from jax.experimental import pallas as pl
from jax.experimental.pallas import tpu as pltpu
from jax.sharding import PartitionSpec as P

QH = 32
KVH = 4
HD = 128
BLK = 128
CHUNKS = 4
HIDE = -1e30

penalty_weight = 0.5
MESH = pl.DeviceIdType.MESH


def project_kernel(
    f, n, wb, hidden, weight, out,
    hid, wts, part, rs, own, kvw,
    hid_send, hid_recv, w_send, w_recv, rs_send, rs_recv, ag_send, ag_recv, local_sem,
):
    rows = hidden.shape[0]
    slab = weight.shape[0]
    cols = weight.shape[1] // CHUNKS
    hs = n // 2
    group = f * hs
    fx = lax.axis_index("fsdp")
    sq = lax.axis_index("seq")
    half = sq // hs
    zz = sq % hs
    gi = fx * hs + zz
    mirror = (1 - half) * hs + zz

    def member(d):
        g = (gi + d) % group
        return g // hs, g % hs

    def hid_slice(mf, mz, side):
        place = jnp.where(side == 0, half, 1 - half)
        start = (mf * n + place * hs + mz) * slab
        return hidden.at[:, pl.ds(pl.multiple_of(start, 128), slab)]

    def hid_copy(d, side):
        mf, mz = member(d)
        return pltpu.make_async_remote_copy(
            src_ref=hid_slice(mf, mz, side),
            dst_ref=hid.at[side, group - d],
            send_sem=hid_send.at[side, d],
            recv_sem=hid_recv.at[side, group - d],
            device_id={"fsdp": mf, "seq": half * hs + mz},
            device_id_type=MESH,
        )

    def hid_arrival(d, side):
        mf, mz = member(d)
        return pltpu.make_async_remote_copy(
            src_ref=hid_slice(mf, mz, side),
            dst_ref=hid.at[side, d],
            send_sem=hid_send.at[side, d],
            recv_sem=hid_recv.at[side, d],
            device_id={"fsdp": mf, "seq": half * hs + mz},
            device_id_type=MESH,
        )

    def w_copy(c):
        return pltpu.make_async_remote_copy(
            src_ref=weight.at[:, c * cols:(c + 1) * cols],
            dst_ref=wts.at[1, c],
            send_sem=w_send.at[c],
            recv_sem=w_recv.at[c],
            device_id={"seq": mirror},
            device_id_type=MESH,
        )

    def rs_copy(c, d):
        mf, mz = member(d)
        return pltpu.make_async_remote_copy(
            src_ref=part.at[c, d],
            dst_ref=rs.at[c, group - d],
            send_sem=rs_send.at[c, d],
            recv_sem=rs_recv.at[c, group - d],
            device_id={"fsdp": mf, "seq": half * hs + mz},
            device_id_type=MESH,
        )

    def rs_arrival(c, d):
        mf, mz = member(d)
        return pltpu.make_async_remote_copy(
            src_ref=part.at[c, d],
            dst_ref=rs.at[c, d],
            send_sem=rs_send.at[c, d],
            recv_sem=rs_recv.at[c, d],
            device_id={"fsdp": mf, "seq": half * hs + mz},
            device_id_type=MESH,
        )

    def ag_copy(c, j):
        return pltpu.make_async_remote_copy(
            src_ref=kvw.at[wb, c],
            dst_ref=kvw.at[wb - j, c],
            send_sem=ag_send.at[c, j - 1],
            recv_sem=ag_recv.at[c, j - 1],
            device_id={"seq": (sq + j) % n},
            device_id_type=MESH,
        )

    own_w = [
        pltpu.make_async_copy(
            weight.at[:, c * cols:(c + 1) * cols], wts.at[0, c], local_sem.at[2 + c]
        )
        for c in range(CHUNKS)
    ]
    own_h = [
        pltpu.make_async_copy(hid_slice(fx, zz, side), hid.at[side, 0], local_sem.at[side])
        for side in range(2)
    ]

    barrier = pltpu.get_barrier_semaphore()
    everyone = f * n
    me = fx * n + sq

    def greet(d, carry):
        other = (me + d) % everyone
        pl.semaphore_signal(
            barrier, inc=1, device_id={"fsdp": other // n, "seq": other % n}, device_id_type=MESH
        )
        return carry

    lax.fori_loop(1, everyone, greet, 0)
    pl.semaphore_wait(barrier, everyone - 1)

    def send_hidden(d, carry):
        hid_copy(d, 0).start()
        hid_copy(d, 1).start()
        return carry

    lax.fori_loop(1, group, send_hidden, 0)
    for c in range(CHUNKS):
        w_copy(c).start()
    for copy in own_h + own_w:
        copy.start()

    for j in range(1, wb + 1):
        @pl.when(sq < j)
        def _():
            kvw[wb - j] = jnp.zeros_like(kvw[wb - j])

    for copy in own_h + own_w:
        copy.wait()

    def take_hidden(d, carry):
        hid_arrival(d, 0).wait_recv()
        hid_arrival(d, 1).wait_recv()
        return carry

    lax.fori_loop(1, group, take_hidden, 0)

    def product(c, d):
        return jnp.dot(hid[0, d], wts[0, c], preferred_element_type=jnp.float32) + jnp.dot(
            hid[1, d], wts[1, c], preferred_element_type=jnp.float32
        )

    def finish(c):
        def add(d, carry):
            rs_arrival(c, d).wait_recv()
            own[c] += rs[c, d].astype(jnp.float32)
            return carry

        lax.fori_loop(1, group, add, 0)
        kvw[wb, c] = own[c].astype(jnp.bfloat16)
        for j in range(1, wb + 1):
            @pl.when(sq + j < n)
            def _():
                ag_copy(c, j).start()

    for c in range(CHUNKS):
        w_copy(c).wait_recv()

        def spread(d, carry):
            part[c, d] = product(c, d).astype(jnp.bfloat16)
            rs_copy(c, d).start()
            return carry

        lax.fori_loop(1, group, spread, 0)
        own[c] = product(c, 0)
        if c > 0:
            finish(c - 1)
    finish(CHUNKS - 1)

    def sent(d, carry):
        hid_copy(d, 0).wait_send()
        hid_copy(d, 1).wait_send()
        for c in range(CHUNKS):
            rs_copy(c, d).wait_send()
        return carry

    lax.fori_loop(1, group, sent, 0)
    for c in range(CHUNKS):
        w_copy(c).wait_send()
        for j in range(1, wb + 1):
            @pl.when(sq >= j)
            def _():
                ag_copy(c, j).wait_recv()

            @pl.when(sq + j < n)
            def _():
                ag_copy(c, j).wait_send()
    for s in range(wb + 1):
        for c in range(CHUNKS):
            out[s * rows:(s + 1) * rows, c * cols:(c + 1) * cols] = kvw[s, c]


def project(hidden, weight, f, n, wb):
    rows = hidden.shape[0]
    slab, width = weight.shape
    group = f * (n // 2)
    cols = width // CHUNKS
    dma = pltpu.SemaphoreType.DMA
    return pl.pallas_call(
        functools.partial(project_kernel, f, n, wb),
        out_shape=jax.ShapeDtypeStruct(((wb + 1) * rows, width), jnp.bfloat16),
        in_specs=[pl.BlockSpec(memory_space=pl.ANY)] * 2,
        out_specs=pl.BlockSpec(memory_space=pltpu.VMEM),
        scratch_shapes=[
            pltpu.VMEM((2, group, rows, slab), jnp.bfloat16),
            pltpu.VMEM((2, CHUNKS, slab, cols), jnp.bfloat16),
            pltpu.VMEM((CHUNKS, group, rows, cols), jnp.bfloat16),
            pltpu.VMEM((CHUNKS, group, rows, cols), jnp.bfloat16),
            pltpu.VMEM((CHUNKS, rows, cols), jnp.float32),
            pltpu.VMEM((wb + 1, CHUNKS, rows, cols), jnp.bfloat16),
            dma((2, group)), dma((2, group)),
            dma((CHUNKS,)), dma((CHUNKS,)),
            dma((CHUNKS, group)), dma((CHUNKS, group)),
            dma((CHUNKS, wb)), dma((CHUNKS, wb)),
            dma((2 + CHUNKS,)),
        ],
        compiler_params=pltpu.CompilerParams(
            collective_id=0, has_side_effects=True, vmem_limit_bytes=56 * 1024 * 1024
        ),
        cost_estimate=pl.CostEstimate(
            flops=2 * group * rows * 2 * slab * width,
            bytes_accessed=2 * rows * hidden.shape[1] + 4 * slab * width,
            transcendentals=0,
        ),
    )(hidden, weight)


def attend_kernel(blocks, first, q, keys, values, gains, q_doc, k_doc, grad, scores, bias):
    rows, window = bias.shape
    heads = gains.shape[0]
    scale = 1.0 / math.sqrt(HD)
    step = pl.program_id(0)

    @pl.when(step == 0)
    def _():
        ahead = window - rows
        for a in range(rows // BLK):
            for b in range(window // BLK):
                own = b == a + ahead // BLK
                if b > a + ahead // BLK:
                    seen = jnp.zeros((BLK, BLK), jnp.bool_)
                else:
                    seen = q_doc[a * BLK:(a + 1) * BLK, :] == k_doc[:, b * BLK:(b + 1) * BLK]
                    if own:
                        i = lax.broadcasted_iota(jnp.int32, (BLK, BLK), 0)
                        j = lax.broadcasted_iota(jnp.int32, (BLK, BLK), 1)
                        seen = seen & (j <= i)
                place = first[0] + b
                bias[a * BLK:(a + 1) * BLK, b * BLK:(b + 1) * BLK] = jnp.where(seen, 0.0, HIDE)
                if b < a + ahead // BLK:
                    shut = (place < 0) | (blocks[a, jnp.maximum(place, 0)] != 1)

                    @pl.when(shut)
                    def _():
                        bias[a * BLK:(a + 1) * BLK, b * BLK:(b + 1) * BLK] = jnp.full(
                            (BLK, BLK), HIDE, jnp.float32
                        )
        scores[...] = jnp.zeros_like(scores)

    k = keys[...]
    gain = lax.dot_general(
        gains[...], values[...].astype(jnp.float32), (((1,), (1,)), ((), ())),
        precision=lax.Precision.HIGHEST, preferred_element_type=jnp.float32,
    )
    total = jnp.zeros((rows, 1), jnp.float32)
    for h in range(heads):
        logits = lax.dot_general(
            q[:, h * HD:(h + 1) * HD], k, (((1,), (1,)), ((), ())),
            preferred_element_type=jnp.float32,
        )
        p = jnp.exp2(logits * (scale * math.log2(math.e)) + bias[...])
        u = gain[h:h + 1, :]
        den = jnp.sum(p, axis=1, keepdims=True)
        inverse = 1.0 / den
        rho = jnp.sum(p * u, axis=1, keepdims=True) * inverse
        pulled = (p * (u - rho)).astype(jnp.bfloat16)
        moved = jnp.dot(pulled, k, preferred_element_type=jnp.float32)
        grad[:, h * HD:(h + 1) * HD] = (moved * (scale * inverse)).astype(grad.dtype)
        total = total + rho
    scores[...] += total


def attend(q, kv, gains, q_doc, k_doc, blocks, first):
    rows, width = q.shape
    window = kv.shape[0]
    group_size = QH // KVH
    smem = pl.BlockSpec(memory_space=pltpu.SMEM)
    return pl.pallas_call(
        attend_kernel,
        grid=(KVH,),
        out_shape=(
            jax.ShapeDtypeStruct((rows, width), jnp.bfloat16),
            jax.ShapeDtypeStruct((rows, 1), jnp.float32),
        ),
        in_specs=[
            smem,
            smem,
            pl.BlockSpec((rows, group_size * HD), lambda s: (0, s)),
            pl.BlockSpec((window, HD), lambda s: (0, s)),
            pl.BlockSpec((window, HD), lambda s: (0, KVH + s)),
            pl.BlockSpec((group_size, HD), lambda s: (s, 0)),
            pl.BlockSpec((rows, 1), lambda s: (0, 0)),
            pl.BlockSpec((1, window), lambda s: (0, 0)),
        ],
        out_specs=(
            pl.BlockSpec((rows, group_size * HD), lambda s: (0, s)),
            pl.BlockSpec((rows, 1), lambda s: (0, 0)),
        ),
        scratch_shapes=[pltpu.VMEM((rows, window), jnp.float32)],
        compiler_params=pltpu.CompilerParams(vmem_limit_bytes=48 * 1024 * 1024),
        cost_estimate=pl.CostEstimate(
            flops=4 * rows * width * window,
            bytes_accessed=4 * rows * width + 2 * window * 2 * KVH * HD,
            transcendentals=rows * window * QH,
        ),
    )(blocks, first, q, kv, kv, gains, q_doc, k_doc)


def on_device(hidden, queries, kv_weight, readout, segments, block_mask, response):
    rows = hidden.shape[1]
    f = lax.axis_size("fsdp")
    n = lax.axis_size("seq")
    seq_len = segments.shape[1]
    wb = -(-(seq_len // 2 - 1) // rows)
    sq = lax.axis_index("seq")
    kv = project(hidden[0], kv_weight[0], f, n, wb)
    docs = jnp.concatenate([jnp.full((1, wb * rows), -1, jnp.int32), segments], axis=1)
    k_doc = lax.dynamic_slice_in_dim(docs, sq * rows, (wb + 1) * rows, 1)
    q_doc = k_doc[:, wb * rows:].reshape(rows, 1)
    first = ((sq - wb) * (rows // BLK)).astype(jnp.int32).reshape(1)
    grad, token_scores = attend(
        queries[0], kv, readout[0].reshape(QH, HD), q_doc, k_doc, block_mask[0], first
    )
    token_scores = token_scores.reshape(1, rows)
    joined = lax.all_gather(token_scores, "section", axis=0, tiled=True)
    section_index = lax.axis_index("section")
    actor_part = (section_index == 0).astype(jnp.float32)
    critic_part = (section_index == 3).astype(jnp.float32)
    live_rows = response.astype(jnp.float32)
    actor_term = penalty_weight * (joined[0] - joined[1]) - (joined[2] - joined[3])
    critic_term = joined[3] - joined[2]
    loss_grad = live_rows * (actor_part * actor_term + critic_part * critic_term)
    query_grad = (loss_grad[:, None] * grad.astype(jnp.float32)).astype(jnp.bfloat16)
    return (token_scores, query_grad[None])


def solution(mesh):
    placed = (
        P("section", ("fsdp", "seq"), None),
        P("section", ("fsdp", "seq"), None),
        P("section", ("fsdp", "seq"), None),
        P("section", None),
        P("fsdp", None),
        P("fsdp", "seq", None),
        P(("fsdp", "seq")),
    )
    return jax.shard_map(
        on_device,
        mesh=mesh,
        in_specs=placed,
        out_specs=(P("section", ("fsdp", "seq")), P("section", ("fsdp", "seq"), None)),
        check_vma=False,
    )
```

time: 405 us -> 177 us (0.44)
  Pallas kernels: 0 us -> 158 us
  blocking collectives: 150 us -> 12.3 us
  matrix products: 91.6 us -> 0 us
  waiting for transfers between devices: 84.3 us -> 0 us
  local copies, waits for them, and re-layouts: 50.7 us -> 2.94 us
  between operations: 14.2 us -> 0.74 us
  other arithmetic: 7.84 us -> 2.72 us
  starting transfers between devices: 4.92 us -> 0 us
    pallas_call x0 -> x2, Pallas kernels: none -> 158 us  [the longest x1 141 us: project(): pl.pallas_call(functools.partial(project_kernel, f, n, wb), out_shape=jax...]
    psum x1 -> x0, blocking collectives: 141 us -> none  [on_device(): whole_kv = lax.psum(partial_kv, 'seq').astype(jnp.bfloat16)]
    dot_general x21 -> x0, matrix products: 91.6 us -> none  [the longest x4 34.7 us: key_block(): jnp.einsum('kgij,jkd->ikgd', rounded, block_values, preferred_element_typ...]
    all_to_all x1 -> x0, waiting for transfers between devices: 83.6 us -> none  [on_device(): lax.all_to_all(split_rows, 'seq', split_axis=2, concat_axis=0, tiled=True)]
    another operation x2 -> x0, local copies, waits for them, and re-layouts: 15.2 us -> none  [on_device(): split_rows = local_rows.reshape(row_count, fsdp_count, seq_count, slab_rows)]
    while x64 -> x0, local copies, waits for them, and re-layouts: 12.9 us -> none
    unnamed x15 -> x10, local copies, waits for them, and re-layouts: 11.3 us -> 1.42 us
    broadcast_in_dim x4 -> x0, local copies, waits for them, and re-layouts: 7.31 us -> none  [the longest x3 7.31 us: on_device(): empty_acc = jnp.zeros((row_count, KVH, group_size, HD), jnp.float32)]
  transfers between devices with their start and end apart: 2 -> 0, of which waited for: 1 -> 0; matrix products, arithmetic and copies ran while one was open for 3% -> 0% of each run, Pallas kernels for 0% -> 0%
where the time goes in v1:
time: 177 us; the launch traced here: 176 us
  Pallas kernels  158 us (89%)
  blocking collectives  12.3 us (7%)
  local copies, waits for them, and re-layouts  2.94 us (2%)
  other arithmetic  2.72 us (2%)
    pallas_call x1, Pallas kernels, project(): pl.pallas_call(functools.partial(project_kernel, f, n, wb), out_shape=jax...  141 us
    pallas_call x1, Pallas kernels, attend(): pl.pallas_call(attend_kernel, grid=(KVH,), out_shape=(jax.ShapeDtypeStruc...  17.1 us
    all_gather x1, blocking collectives, on_device(): joined = lax.all_gather(token_scores, 'section', axis=0, tiled=True)  12.3 us

profile of v1, /device:TPU:25, one launch (start us, length us, event | category | flops | bytes accessed | tf_op | source)
XLA Modules:
  0.0 176.3 jit_solution(7351496760528331790)
XLA Ops:
  0.6 0.7 fusion.6
  1.3 0.7 pad_dynamic-slice_fusion.1.k_doc
  2.0 0.1 copy.10.q_doc
  2.2 0.0 copy-start
  2.2 0.0 copy-start.1
  2.2 0.0 copy-start.2
  2.2 140.6 %shard_map.86.keys.values = bf16[768,1024]{1,0:T(8,128)(2,1)} custom-call(bf16[256,8192]{1,0:T(8,128)(2,1)} %bitcast.15, bf16[1024,1024]{1,0:T(8,128)(2,1)} %bitcast.16), custom_call_target="tpu_custom_call" | custom-call | flops 4294967296 | bytes 8388608 | tf_op jit(solution)/shard_map/pallas_call | solution.py:224
  142.8 0.0 copy-done
  142.8 0.0 copy-done.1
  142.8 0.0 copy-done.2
  142.8 0.0 copy-start.3
  142.9 1.4 copy-done.3
  144.3 0.0 copy-start.4
  144.3 17.1 %shard_map.87 = (bf16[256,4096]{1,0:T(8,128)(2,1)S(1)}, f32[256,1]{1,0:T(8,128)S(1)}) custom-call(s32[2,8]{1,0:T(2,128)S(1)} %bitcast.13, s32[1]{0:T(128)} %bitcast.1.first, bf16[256,4096]{1,0:T(8,128)(2,1)S(1)} %bitcast.11, bf16[768,1024]{1,0:T(8,128)(2,1)S(1)} %copy-done.3, bf16[768,1024]{1,0:T(8,128)(2,1)S(1)} %copy-done.3, f32[32,128]{1,0:T(8,128)S(1)} %bitcast.12, ...), custom_call_target="tpu_custom_call" | custom-call | flops 3221225472 | bytes 5767168 | tf_op jit(solution)/shard_map/pallas_call | solution.py:313
  161.4 0.7 reduce
  162.0 12.3 %all-gather = f32[1024,1]{1,0:T(8,128)S(1)} all-gather(f32[256,1]{1,0:T(8,128)S(1)} %get-tuple-element.4), channel_id=2, replica_groups=mesh['section'=4,'fsdp'=2,'seq'=4] {'section'}, dimensions={0}, use_global_device_ids=true | all-gather | bytes 5120 | tf_op jit(solution)/shard_map/all_gather | solution.py:360
  174.3 0.1 fusion.5
  174.4 0.0 copy-done.4
  174.4 1.9 %fusion = bf16[1,256,4096]{2,1,0:T(8,128)(2,1)} fusion(bf16[256,4096]{1,0:T(8,128)(2,1)S(1)} %get-tuple-element.5, f32[256]{0:T(256)S(1)} %convert_multiply_fusion), kind=kLoop, calls=%fused_computation.1 | loop fusion | flops 3145728 | bytes 4195328 | tf_op jit(solution)/shard_map/broadcast_in_dim | solution.py:369
  (1 shorter events, 0.0 us)
Async XLA Ops:
  2.2 140.7 %copy-start = (bf16[1,256,4096]{2,1,0:T(8,128)(2,1)S(1)}, bf16[1,256,4096]{2,1,0:T(8,128)(2,1)}, u32[]{:S(2)}) copy-start(bf16[1,256,4096]{2,1,0:T(8,128)(2,1)} %param.8) | copy-start | bytes 6291460
  2.2 140.7 %copy-start.1 = (f32[1,4096]{1,0:T(1,128)S(1)}, f32[1,4096]{1,0:T(1,128)}, u32[]{:S(2)}) copy-start(f32[1,4096]{1,0:T(1,128)} %param.10) | copy-start | bytes 49156
  2.2 140.6 %copy-start.2 = (s32[1,2,8]{2,1,0:T(2,128)S(1)}, s32[1,2,8]{2,1,0:T(2,128)}, u32[]{:S(2)}) copy-start(s32[1,2,8]{2,1,0:T(2,128)} %param.12) | copy-start | bytes 196
  142.8 1.4 copy-start.3
  144.3 30.2 %copy-start.4 = (s32[256]{0:T(256)S(1)}, s32[256]{0:T(256)}, u32[]{:S(2)}) copy-start(s32[256]{0:T(256)} %param.13) | copy-start | bytes 3076

commit v2 on v1

v2 whole, which is shorter than its diff:
```python
import functools
import math

import jax
import jax.numpy as jnp
from jax import lax
from jax.experimental import pallas as pl
from jax.experimental.pallas import tpu as pltpu
from jax.sharding import PartitionSpec as P

QH = 32
KVH = 4
HD = 128
BLK = 128
CHUNKS = KVH
HIDE = -1e30

penalty_weight = 0.5
MESH = pl.DeviceIdType.MESH


def step_kernel(
    f, n, wb, sections, hidden, weight, queries, gains, q_doc, k_doc, opened, live,
    grad, scores, factor,
    hid, wts, part, rs, own, kvw, q, moved, bias, gain, joined,
    hid_send, hid_recv, w_send, w_recv, rs_send, rs_recv, ag_send, ag_recv,
    join_send, join_recv, local_sem, grad_sem,
):
    rows = hidden.shape[0]
    slab = weight.shape[0]
    cols = weight.shape[1] // CHUNKS
    hs = n // 2
    group = f * hs
    fx = lax.axis_index("fsdp")
    sq = lax.axis_index("seq")
    half = sq // hs
    zz = sq % hs
    gi = fx * hs + zz
    mirror = (1 - half) * hs + zz
    sec = lax.axis_index("section")

    def member(d):
        g = (gi + d) % group
        return g // hs, g % hs

    def hid_slice(mf, mz, side):
        place = jnp.where(side == 0, half, 1 - half)
        start = (mf * n + place * hs + mz) * slab
        return hidden.at[:, pl.ds(pl.multiple_of(start, 128), slab)]

    def hid_copy(d, side):
        mf, mz = member(d)
        return pltpu.make_async_remote_copy(
            src_ref=hid_slice(mf, mz, side),
            dst_ref=hid.at[side, group - d],
            send_sem=hid_send.at[side, d],
            recv_sem=hid_recv.at[side, group - d],
            device_id={"fsdp": mf, "seq": half * hs + mz},
            device_id_type=MESH,
        )

    def hid_arrival(d, side):
        mf, mz = member(d)
        return pltpu.make_async_remote_copy(
            src_ref=hid_slice(mf, mz, side),
            dst_ref=hid.at[side, d],
            send_sem=hid_send.at[side, d],
            recv_sem=hid_recv.at[side, d],
            device_id={"fsdp": mf, "seq": half * hs + mz},
            device_id_type=MESH,
        )

    def w_slice(c, t):
        start = (t * KVH + c) * HD
        return weight.at[:, start:start + HD]

    def w_copy(c, t):
        return pltpu.make_async_remote_copy(
            src_ref=w_slice(c, t),
            dst_ref=wts.at[1, c, :, t * HD:(t + 1) * HD],
            send_sem=w_send.at[c, t],
            recv_sem=w_recv.at[c, t],
            device_id={"seq": mirror},
            device_id_type=MESH,
        )

    def rs_copy(c, d):
        mf, mz = member(d)
        return pltpu.make_async_remote_copy(
            src_ref=part.at[c, d],
            dst_ref=rs.at[c, group - d],
            send_sem=rs_send.at[c, d],
            recv_sem=rs_recv.at[c, group - d],
            device_id={"fsdp": mf, "seq": half * hs + mz},
            device_id_type=MESH,
        )

    def rs_arrival(c, d):
        mf, mz = member(d)
        return pltpu.make_async_remote_copy(
            src_ref=part.at[c, d],
            dst_ref=rs.at[c, d],
            send_sem=rs_send.at[c, d],
            recv_sem=rs_recv.at[c, d],
            device_id={"fsdp": mf, "seq": half * hs + mz},
            device_id_type=MESH,
        )

    def ag_copy(c, j):
        return pltpu.make_async_remote_copy(
            src_ref=kvw.at[wb, c],
            dst_ref=kvw.at[wb - j, c],
            send_sem=ag_send.at[c, j - 1],
            recv_sem=ag_recv.at[c, j - 1],
            device_id={"seq": (sq + j) % n},
            device_id_type=MESH,
        )

    own_w = [
        pltpu.make_async_copy(
            w_slice(c, t), wts.at[0, c, :, t * HD:(t + 1) * HD], local_sem.at[2 + 2 * c + t]
        )
        for c in range(CHUNKS)
        for t in range(2)
    ]
    own_q = pltpu.make_async_copy(queries, q, local_sem.at[2 + 2 * CHUNKS])

    def join_copy(d):
        return pltpu.make_async_remote_copy(
            src_ref=joined.at[sec],
            dst_ref=joined.at[sec],
            send_sem=join_send.at[d],
            recv_sem=join_recv.at[sections - d],
            device_id={"section": (sec + d) % sections},
            device_id_type=MESH,
        )

    def join_arrival(d):
        return pltpu.make_async_remote_copy(
            src_ref=joined.at[sec],
            dst_ref=joined.at[(sec + d) % sections],
            send_sem=join_send.at[d],
            recv_sem=join_recv.at[d],
            device_id={"section": (sec + d) % sections},
            device_id_type=MESH,
        )

    def grad_copy(c):
        wide = gains.shape[0] // KVH * HD
        return pltpu.make_async_copy(
            moved.at[c], grad.at[:, c * wide:(c + 1) * wide], grad_sem.at[c]
        )

    own_h = [
        pltpu.make_async_copy(hid_slice(fx, zz, side), hid.at[side, 0], local_sem.at[side])
        for side in range(2)
    ]

    barrier = pltpu.get_barrier_semaphore()
    everyone = f * n
    me = fx * n + sq

    def greet(d, carry):
        other = (me + d) % everyone
        pl.semaphore_signal(
            barrier, inc=1, device_id={"fsdp": other // n, "seq": other % n}, device_id_type=MESH
        )
        return carry

    lax.fori_loop(1, everyone, greet, 0)
    for d in range(1, sections):
        pl.semaphore_signal(
            barrier, inc=1, device_id={"section": (sec + d) % sections}, device_id_type=MESH
        )
    pl.semaphore_wait(barrier, everyone - 1 + sections - 1)

    def send_hidden(d, carry):
        hid_copy(d, 0).start()
        hid_copy(d, 1).start()
        return carry

    lax.fori_loop(1, group, send_hidden, 0)
    for c in range(CHUNKS):
        w_copy(c, 0).start()
        w_copy(c, 1).start()
    for copy in own_h + own_w + [own_q]:
        copy.start()

    window = (wb + 1) * rows
    i = lax.broadcasted_iota(jnp.int32, (BLK, window), 0)
    j = lax.broadcasted_iota(jnp.int32, (BLK, window), 1) - wb * rows
    for a in range(rows // BLK):
        seen = q_doc[a * BLK:(a + 1) * BLK, :] == k_doc[...]
        seen = seen & (j <= i + a * BLK)
        seen = seen & ((opened[a:a + 1, :] == 1) | (j >= a * BLK))
        bias[a * BLK:(a + 1) * BLK, :] = jnp.where(seen, 0.0, HIDE)

    for j in range(1, wb + 1):
        @pl.when(sq < j)
        def _():
            kvw[wb - j] = jnp.zeros_like(kvw[wb - j])

    for copy in own_h + own_w + [own_q]:
        copy.wait()

    def take_hidden(d, carry):
        hid_arrival(d, 0).wait_recv()
        hid_arrival(d, 1).wait_recv()
        return carry

    lax.fori_loop(1, group, take_hidden, 0)

    def product(c, d):
        return jnp.dot(hid[0, d], wts[0, c], preferred_element_type=jnp.float32) + jnp.dot(
            hid[1, d], wts[1, c], preferred_element_type=jnp.float32
        )

    def finish(c):
        def add(d, carry):
            rs_arrival(c, d).wait_recv()
            own[c] += rs[c, d].astype(jnp.float32)
            return carry

        lax.fori_loop(1, group, add, 0)
        kvw[wb, c] = own[c].astype(jnp.bfloat16)
        for j in range(1, wb + 1):
            @pl.when(sq + j < n)
            def _():
                ag_copy(c, j).start()

    scale = 1.0 / math.sqrt(HD)
    heads = gains.shape[0] // KVH

    def attend(c, total):
        for j in range(1, wb + 1):
            @pl.when(sq >= j)
            def _():
                ag_copy(c, j).wait_recv()

        k = kvw[:, c, :, :HD].reshape(window, HD)
        v = kvw[:, c, :, HD:].reshape(window, HD)
        gain[...] = lax.dot_general(
            gains[c * heads:(c + 1) * heads, :], v.astype(jnp.float32), (((1,), (1,)), ((), ())),
            precision=lax.Precision.HIGHEST, preferred_element_type=jnp.float32,
        )

        def head(h, total):
            start = pl.multiple_of((c * heads + h) * HD, HD)
            logits = lax.dot_general(
                q[:, pl.ds(start, HD)], k, (((1,), (1,)), ((), ())),
                preferred_element_type=jnp.float32,
            )
            p = jnp.exp2(logits * (scale * math.log2(math.e)) + bias[...])
            u = gain[pl.ds(h, 1), :]
            inverse = 1.0 / jnp.sum(p, axis=1, keepdims=True)
            rho = jnp.sum(p * u, axis=1, keepdims=True) * inverse
            pulled = (p * (u - rho)).astype(jnp.bfloat16)
            pull = jnp.dot(pulled, k, preferred_element_type=jnp.float32) * (scale * inverse)
            moved[c, :, pl.ds(pl.multiple_of(h * HD, HD), HD)] = pull.astype(jnp.bfloat16)
            return total + rho

        def pair(t, total):
            return head(2 * t + 1, head(2 * t, total))

        total = lax.fori_loop(0, heads // 2, pair, total)
        grad_copy(c).start()
        return total

    total = jnp.zeros((rows, 1), jnp.float32)
    for c in range(CHUNKS):
        w_copy(c, 0).wait_recv()
        w_copy(c, 1).wait_recv()

        def spread(d, carry):
            part[c, d] = product(c, d).astype(jnp.bfloat16)
            rs_copy(c, d).start()
            return carry

        lax.fori_loop(1, group, spread, 0)
        own[c] = product(c, 0)
        if c > 0:
            finish(c - 1)
        if c > 1:
            total = attend(c - 2, total)
    finish(CHUNKS - 1)
    total = attend(CHUNKS - 2, total)
    total = attend(CHUNKS - 1, total)

    row = jnp.transpose(jnp.broadcast_to(total, (rows, HD)))[:8, :]
    joined[sec] = row
    scores[...] = row[:1, :]
    for d in range(1, sections):
        join_copy(d).start()

    def sent(d, carry):
        hid_copy(d, 0).wait_send()
        hid_copy(d, 1).wait_send()
        for c in range(CHUNKS):
            rs_copy(c, d).wait_send()
        return carry

    lax.fori_loop(1, group, sent, 0)
    for c in range(CHUNKS):
        w_copy(c, 0).wait_send()
        w_copy(c, 1).wait_send()
        grad_copy(c).wait()
        for j in range(1, wb + 1):
            @pl.when(sq + j < n)
            def _():
                ag_copy(c, j).wait_send()
    for d in range(1, sections):
        join_copy(d).wait_send()
        join_arrival(d).wait_recv()
    by_model = [joined[m, :1, :] for m in range(4)]
    actor_part = (sec == 0).astype(jnp.float32)
    critic_part = (sec == 3).astype(jnp.float32)
    actor_term = penalty_weight * (by_model[0] - by_model[1]) - (by_model[2] - by_model[3])
    critic_term = by_model[3] - by_model[2]
    factor[...] = live[...].astype(jnp.float32) * (
        actor_part * actor_term + critic_part * critic_term
    )


def run_step(hidden, weight, queries, gains, q_doc, k_doc, opened, live, f, n, wb, sections):
    rows = hidden.shape[0]
    slab, width = weight.shape
    group = f * (n // 2)
    cols = width // CHUNKS
    window = (wb + 1) * rows
    wide = queries.shape[1] // KVH
    dma = pltpu.SemaphoreType.DMA
    hbm = pl.BlockSpec(memory_space=pl.ANY)
    vmem = pl.BlockSpec(memory_space=pltpu.VMEM)
    return pl.pallas_call(
        functools.partial(step_kernel, f, n, wb, sections),
        out_shape=(
            jax.ShapeDtypeStruct(queries.shape, jnp.bfloat16),
            jax.ShapeDtypeStruct((1, rows), jnp.float32),
            jax.ShapeDtypeStruct((1, rows), jnp.float32),
        ),
        in_specs=[hbm] * 3 + [vmem] * 5,
        out_specs=(hbm, vmem, vmem),
        scratch_shapes=[
            pltpu.VMEM((2, group, rows, slab), jnp.bfloat16),
            pltpu.VMEM((2, CHUNKS, slab, cols), jnp.bfloat16),
            pltpu.VMEM((CHUNKS, group, rows, cols), jnp.bfloat16),
            pltpu.VMEM((CHUNKS, group, rows, cols), jnp.bfloat16),
            pltpu.VMEM((CHUNKS, rows, cols), jnp.float32),
            pltpu.VMEM((wb + 1, CHUNKS, rows, cols), jnp.bfloat16),
            pltpu.VMEM(queries.shape, jnp.bfloat16),
            pltpu.VMEM((KVH, rows, wide), jnp.bfloat16),
            pltpu.VMEM((rows, window), jnp.float32),
            pltpu.VMEM((QH // KVH, window), jnp.float32),
            pltpu.VMEM((sections, 8, rows), jnp.float32),
            dma((2, group)), dma((2, group)),
            dma((CHUNKS, 2)), dma((CHUNKS, 2)),
            dma((CHUNKS, group)), dma((CHUNKS, group)),
            dma((CHUNKS, wb)), dma((CHUNKS, wb)),
            dma((sections,)), dma((sections,)),
            dma((3 + 2 * CHUNKS,)), dma((KVH,)),
        ],
        compiler_params=pltpu.CompilerParams(
            collective_id=0, has_side_effects=True, vmem_limit_bytes=58 * 1024 * 1024
        ),
        cost_estimate=pl.CostEstimate(
            flops=4 * group * rows * slab * width + 4 * rows * queries.shape[1] * window,
            bytes_accessed=2 * hidden.size + 4 * weight.size + 4 * queries.size,
            transcendentals=rows * window * QH,
        ),
    )(hidden, weight, queries, gains, q_doc, k_doc, opened, live)


def on_device(hidden, queries, kv_weight, readout, segments, block_mask, response):
    rows = hidden.shape[1]
    f = lax.axis_size("fsdp")
    n = lax.axis_size("seq")
    sections = lax.axis_size("section")
    seq_len = segments.shape[1]
    wb = -(-(seq_len // 2 - 1) // rows)
    sq = lax.axis_index("seq")
    docs = jnp.concatenate([jnp.full((1, wb * rows), -1, jnp.int32), segments], axis=1)
    k_doc = lax.dynamic_slice_in_dim(docs, sq * rows, (wb + 1) * rows, 1)
    q_doc = k_doc[:, wb * rows:].reshape(rows, 1)
    table = jnp.repeat(jnp.pad(block_mask[0], ((0, 0), (wb * rows // BLK, 0))), BLK, axis=1)
    opened = lax.dynamic_slice_in_dim(table, sq * rows, (wb + 1) * rows, 1)
    grad, token_scores, factor = run_step(
        hidden[0], kv_weight[0], queries[0], readout[0].reshape(QH, HD),
        q_doc, k_doc, opened, response.reshape(1, rows), f, n, wb, sections,
    )
    query_grad = (factor.reshape(rows, 1) * grad.astype(jnp.float32)).astype(jnp.bfloat16)
    return (token_scores, query_grad[None])


def solution(mesh):
    placed = (
        P("section", ("fsdp", "seq"), None),
        P("section", ("fsdp", "seq"), None),
        P("section", ("fsdp", "seq"), None),
        P("section", None),
        P("fsdp", None),
        P("fsdp", "seq", None),
        P(("fsdp", "seq")),
    )
    return jax.shard_map(
        on_device,
        mesh=mesh,
        in_specs=placed,
        out_specs=(P("section", ("fsdp", "seq")), P("section", ("fsdp", "seq"), None)),
        check_vma=False,
    )
```

time: 177 us -> 163 us (0.921)
  blocking collectives: 12.3 us -> 0 us
  Pallas kernels: 158 us -> 153 us
  local copies, waits for them, and re-layouts: 2.94 us -> 4.77 us
    all_gather x1 -> x0, blocking collectives: 12.3 us -> none  [on_device(): joined = lax.all_gather(token_scores, 'section', axis=0, tiled=True)]
    pallas_call x2 -> x1, Pallas kernels: 158 us -> 153 us  [run_step(): pl.pallas_call(functools.partial(step_kernel, f, n, wb, sections), out_sh...]
where the time goes in v2:
time: 163 us; the launch traced here: 162 us
  Pallas kernels  153 us (94%)
  local copies, waits for them, and re-layouts  4.77 us (3%)
  other arithmetic  3.56 us (2%)
    pallas_call x1, Pallas kernels, run_step(): pl.pallas_call(functools.partial(step_kernel, f, n, wb, sections), out_sh...  153 us
    broadcast_in_dim x1, other arithmetic, on_device(): return (token_scores, query_grad[None])  3.56 us

profile of v2, /device:TPU:25, one launch (start us, length us, event | category | flops | bytes accessed | tf_op | source)
XLA Modules:
  0.0 162.4 jit_solution(17423760248609163676)
XLA Ops:
  0.6 0.7 fusion.1
  1.3 0.8 pad.5
  2.1 1.3 pad_dynamic-slice_fusion.1.k_doc
  3.4 0.1 broadcast_bitcast_fusion
  3.4 0.6 constant_dynamic-slice_fusion.opened
  4.0 0.8 copy.9.q_doc
  4.8 153.5 %shard_map.86 = (bf16[256,4096]{1,0:T(8,128)(2,1)}, f32[1,256]{1,0:T(1,128)}, f32[1,256]{1,0:T(1,128)}) custom-call(bf16[256,8192]{1,0:T(8,128)(2,1)} %bitcast.19, bf16[1024,1024]{1,0:T(8,128)(2,1)} %bitcast.20, bf16[256,4096]{1,0:T(8,128)(2,1)} %bitcast.21, f32[32,128]{1,0:T(8,128)} %bitcast.22, s32[256,1]{1,0:T(8,128)} %copy.9.q_doc, ...), custom_call_target="tpu_custom_call" | custom-call | flops 7516192768 | bytes 12582912 | tf_op jit(solution)/shard_map/pallas_call | solution.py:334
  158.3 0.0 copy-start
  158.3 3.6 %fusion = bf16[1,256,4096]{2,1,0:T(8,128)(2,1)} fusion(bf16[256,4096]{1,0:T(8,128)(2,1)} %get-tuple-element.7, f32[256]{0:T(256)} %bitcast.17), kind=kLoop, calls=%fused_computation.1 | loop fusion | flops 3145728 | bytes 4195328 | tf_op jit(solution)/shard_map/broadcast_in_dim | solution.py:391
  161.9 0.0 copy-done
  161.9 0.6 copy.14
  (1 shorter events, 0.0 us)
Async XLA Ops:
  158.3 3.6 %copy-start = (f32[1,256]{1,0:T(1,128)S(1)}, f32[1,256]{1,0:T(1,128)}, u32[]{:S(2)}) copy-start(f32[1,256]{1,0:T(1,128)} %get-tuple-element.10) | copy-start | bytes 3076

commit v3 on v2

--- a/solution.py
+++ b/solution.py
@@ -22,8 +22,8 @@
 def step_kernel(
     f, n, wb, sections, hidden, weight, queries, gains, q_doc, k_doc, opened, live,
     grad, scores, factor,
-    hid, wts, part, rs, own, kvw, q, moved, bias, gain, joined,
-    hid_send, hid_recv, w_send, w_recv, rs_send, rs_recv, ag_send, ag_recv,
+    hid, wts, part, rs, part2, rs2, own, kvw, q, moved, bias, gain, joined,
+    hid_send, hid_recv, w_send, w_recv, rs_send, rs_recv, al_send, al_recv, ag_send, ag_recv,
     join_send, join_recv, local_sem, grad_sem,
 ):
     rows = hidden.shape[0]
@@ -84,25 +84,30 @@
             device_id_type=MESH,
         )
 
-    def rs_copy(c, d):
-        mf, mz = member(d)
-        return pltpu.make_async_remote_copy(
-            src_ref=part.at[c, d],
-            dst_ref=rs.at[c, group - d],
-            send_sem=rs_send.at[c, d],
-            recv_sem=rs_recv.at[c, group - d],
-            device_id={"fsdp": mf, "seq": half * hs + mz},
-            device_id_type=MESH,
-        )
-
-    def rs_arrival(c, d):
-        mf, mz = member(d)
-        return pltpu.make_async_remote_copy(
-            src_ref=part.at[c, d],
-            dst_ref=rs.at[c, d],
-            send_sem=rs_send.at[c, d],
-            recv_sem=rs_recv.at[c, d],
-            device_id={"fsdp": mf, "seq": half * hs + mz},
+    def rs_move(c, e, slot):
+        df, dz = e // hs, e % hs
+        return pltpu.make_async_remote_copy(
+            src_ref=part.at[c, e - hs],
+            dst_ref=rs.at[c, slot - hs],
+            send_sem=rs_send.at[c, e - hs],
+            recv_sem=rs_recv.at[c, slot - hs],
+            device_id={"fsdp": (fx + df) % f},
+            device_id_type=MESH,
+        )
+
+    def rs_copy(c, e):
+        return rs_move(c, e, (f - e // hs) * hs + e % hs)
+
+    def rs_arrival(c, e):
+        return rs_move(c, e, e)
+
+    def along_move(c, dz, slot):
+        return pltpu.make_async_remote_copy(
+            src_ref=part2.at[c, dz],
+            dst_ref=rs2.at[c, slot],
+            send_sem=al_send.at[c, dz],
+            recv_sem=al_recv.at[c, slot],
+            device_id={"seq": half * hs + (zz + dz) % hs},
             device_id_type=MESH,
         )
 
@@ -215,14 +220,22 @@
             hid[1, d], wts[1, c], preferred_element_type=jnp.float32
         )
 
+    def middle(c):
+        def add(e, carry):
+            rs_arrival(c, e).wait_recv()
+            own[c, e % hs] += rs[c, e - hs].astype(jnp.float32)
+            return carry
+
+        lax.fori_loop(hs, group, add, 0)
+        for dz in range(1, hs):
+            part2[c, dz] = own[c, dz].astype(jnp.bfloat16)
+            along_move(c, dz, hs - dz).start()
+
     def finish(c):
-        def add(d, carry):
-            rs_arrival(c, d).wait_recv()
-            own[c] += rs[c, d].astype(jnp.float32)
-            return carry
-
-        lax.fori_loop(1, group, add, 0)
-        kvw[wb, c] = own[c].astype(jnp.bfloat16)
+        for dz in range(1, hs):
+            along_move(c, dz, dz).wait_recv()
+            own[c, 0] += rs2[c, dz].astype(jnp.float32)
+        kvw[wb, c] = own[c, 0].astype(jnp.bfloat16)
         for j in range(1, wb + 1):
             @pl.when(sq + j < n)
             def _():
@@ -271,15 +284,25 @@
         w_copy(c, 0).wait_recv()
         w_copy(c, 1).wait_recv()
 
-        def spread(d, carry):
-            part[c, d] = product(c, d).astype(jnp.bfloat16)
-            rs_copy(c, d).start()
+        def place(e):
+            g = (fx + e // hs) % f * hs + (zz + e % hs) % hs
+            return (g - gi + group) % group
+
+        def spread(e, carry):
+            part[c, e - hs] = product(c, place(e)).astype(jnp.bfloat16)
+            rs_copy(c, e).start()
             return carry
 
-        lax.fori_loop(1, group, spread, 0)
-        own[c] = product(c, 0)
+        lax.fori_loop(hs, group, spread, 0)
+
+        def keep(e, carry):
+            own[c, e] = product(c, place(e))
+            return carry
+
+        lax.fori_loop(0, hs, keep, 0)
         if c > 0:
             finish(c - 1)
+        middle(c)
         if c > 1:
             total = attend(c - 2, total)
     finish(CHUNKS - 1)
@@ -295,15 +318,22 @@
     def sent(d, carry):
         hid_copy(d, 0).wait_send()
         hid_copy(d, 1).wait_send()
+        return carry
+
+    lax.fori_loop(1, group, sent, 0)
+
+    def summed(e, carry):
         for c in range(CHUNKS):
-            rs_copy(c, d).wait_send()
+            rs_copy(c, e).wait_send()
         return carry
 
-    lax.fori_loop(1, group, sent, 0)
+    lax.fori_loop(hs, group, summed, 0)
     for c in range(CHUNKS):
         w_copy(c, 0).wait_send()
         w_copy(c, 1).wait_send()
         grad_copy(c).wait()
+        for dz in range(1, hs):
+            along_move(c, dz, hs - dz).wait_send()
         for j in range(1, wb + 1):
             @pl.when(sq + j < n)
             def _():
@@ -324,7 +354,8 @@
 def run_step(hidden, weight, queries, gains, q_doc, k_doc, opened, live, f, n, wb, sections):
     rows = hidden.shape[0]
     slab, width = weight.shape
-    group = f * (n // 2)
+    hs = n // 2
+    group = f * hs
     cols = width // CHUNKS
     window = (wb + 1) * rows
     wide = queries.shape[1] // KVH
@@ -343,9 +374,11 @@
         scratch_shapes=[
             pltpu.VMEM((2, group, rows, slab), jnp.bfloat16),
             pltpu.VMEM((2, CHUNKS, slab, cols), jnp.bfloat16),
-            pltpu.VMEM((CHUNKS, group, rows, cols), jnp.bfloat16),
-            pltpu.VMEM((CHUNKS, group, rows, cols), jnp.bfloat16),
-            pltpu.VMEM((CHUNKS, rows, cols), jnp.float32),
+            pltpu.VMEM((CHUNKS, group - hs, rows, cols), jnp.bfloat16),
+            pltpu.VMEM((CHUNKS, group - hs, rows, cols), jnp.bfloat16),
+            pltpu.VMEM((CHUNKS, hs, rows, cols), jnp.bfloat16),
+            pltpu.VMEM((CHUNKS, hs, rows, cols), jnp.bfloat16),
+            pltpu.VMEM((CHUNKS, hs, rows, cols), jnp.float32),
             pltpu.VMEM((wb + 1, CHUNKS, rows, cols), jnp.bfloat16),
             pltpu.VMEM(queries.shape, jnp.bfloat16),
             pltpu.VMEM((KVH, rows, wide), jnp.bfloat16),
@@ -354,7 +387,8 @@
             pltpu.VMEM((sections, 8, rows), jnp.float32),
             dma((2, group)), dma((2, group)),
             dma((CHUNKS, 2)), dma((CHUNKS, 2)),
-            dma((CHUNKS, group)), dma((CHUNKS, group)),
+            dma((CHUNKS, group - hs)), dma((CHUNKS, group - hs)),
+            dma((CHUNKS, hs)), dma((CHUNKS, hs)),
             dma((CHUNKS, wb)), dma((CHUNKS, wb)),
             dma((sections,)), dma((sections,)),
             dma((3 + 2 * CHUNKS,)), dma((KVH,)),

time: 163 us -> 160 us (0.982)
  Pallas kernels: 153 us -> 151 us
    pallas_call x1, Pallas kernels: 153 us -> 151 us  [run_step(): pl.pallas_call(functools.partial(step_kernel, f, n, wb, sections), out_sh...]
where the time goes in v3:
time: 160 us
  Pallas kernels  151 us (94%)
  local copies, waits for them, and re-layouts  4.77 us (3%)
  other arithmetic  3.56 us (2%)
    pallas_call x1, Pallas kernels, run_step(): pl.pallas_call(functools.partial(step_kernel, f, n, wb, sections), out_sh...  151 us
    broadcast_in_dim x1, other arithmetic, on_device(): return (token_scores, query_grad[None])  3.56 us

profile of v3, /device:TPU:25, one launch (start us, length us, event | category | flops | bytes accessed | tf_op | source)
XLA Modules:
  0.0 159.9 jit_solution(17828775970912422699)
XLA Ops:
  0.6 0.7 fusion.1
  1.3 0.8 pad.5
  2.1 1.3 pad_dynamic-slice_fusion.1.k_doc
  3.4 0.1 broadcast_bitcast_fusion
  3.4 0.6 constant_dynamic-slice_fusion.opened
  4.0 0.8 copy.9.q_doc
  4.8 150.9 %shard_map.86 = (bf16[256,4096]{1,0:T(8,128)(2,1)}, f32[1,256]{1,0:T(1,128)}, f32[1,256]{1,0:T(1,128)}) custom-call(bf16[256,8192]{1,0:T(8,128)(2,1)} %bitcast.19, bf16[1024,1024]{1,0:T(8,128)(2,1)} %bitcast.20, bf16[256,4096]{1,0:T(8,128)(2,1)} %bitcast.21, f32[32,128]{1,0:T(8,128)} %bitcast.22, s32[256,1]{1,0:T(8,128)} %copy.9.q_doc, ...), custom_call_target="tpu_custom_call" | custom-call | flops 7516192768 | bytes 12582912 | tf_op jit(solution)/shard_map/pallas_call | solution.py:365
  155.8 0.0 copy-start
  155.8 3.6 %fusion = bf16[1,256,4096]{2,1,0:T(8,128)(2,1)} fusion(bf16[256,4096]{1,0:T(8,128)(2,1)} %get-tuple-element.7, f32[256]{0:T(256)} %bitcast.17), kind=kLoop, calls=%fused_computation.1 | loop fusion | flops 3145728 | bytes 4195328 | tf_op jit(solution)/shard_map/broadcast_in_dim | solution.py:425
  159.4 0.0 copy-done
  159.4 0.6 copy.14
  (1 shorter events, 0.0 us)
Async XLA Ops:
  155.8 3.6 %copy-start = (f32[1,256]{1,0:T(1,128)S(1)}, f32[1,256]{1,0:T(1,128)}, u32[]{:S(2)}) copy-start(f32[1,256]{1,0:T(1,128)} %get-tuple-element.10) | copy-start | bytes 3076
